TPU v7x, 128 devices: a whole 4x4x4 slice. The times are simulated.
128 devices in a mesh: ab: 32 (over x, z, y_lo), cd: 4 (over y_hi, core).
Axes of the slice: x: 4, y: 4 (y_hi: 2, y_lo: 2; y = y_hi * 2 + y_lo), z: 4, core: 2. Of those that a mesh axis runs over, the one named last changes fastest.
Arguments:
- integrals: bfloat16 [96, 96, 128, 512], P('ab', None, None, 'cd'), may hold values from -0.0234375 to 0.0234375
- amplitudes: bfloat16 [16, 512, 512], P(None, 'ab', 'cd'), may hold values from -6 to 6
- block_sizes: int32 [4], replicated, may hold values from 1 to 128, 500 in all
Outputs:
- symmetric_residual: float32 [16, 96, 96], P(None, 'ab')
Inputs may be any that keep to these rules, and one draw needn't show every extreme that they name: `block_sizes`: the sizes sum to 500 and the largest is exactly 128.
All inputs are finite; a program needn't handle non-finite values.
Results may differ from a plain program's by a relative error of at most 0.0003.
Values may be sent and summed in bfloat16 or wider, within the bound.
A program may use at most 64 MiB of HBM per device.

v0:
```python
import jax
import jax.numpy as jnp
from jax import lax
from jax.sharding import PartitionSpec as P

IRREPS = 4
BLK = 128


def occupied_slots(block_sizes, first_slot, count):
    slot_ids = first_slot + jnp.arange(count, dtype=jnp.int32)
    irrep_ids = slot_ids // BLK
    owners = jnp.arange(IRREPS, dtype=jnp.int32)
    limits = jnp.sum(
        jnp.where(irrep_ids[:, None] == owners[None, :], block_sizes[None, :], 0), axis=1
    )
    return slot_ids % BLK < limits


def on_device(integrals, amplitudes, block_sizes):
    a_count = integrals.shape[0]
    window = integrals.shape[1]
    per_irrep = window // IRREPS
    c_rows = amplitudes.shape[1]
    own_block = lax.axis_index("cd")
    row_first = lax.axis_index("ab") * a_count
    keep_rows = occupied_slots(block_sizes, lax.axis_index("ab") * c_rows, c_rows)
    keep_cols = occupied_slots(block_sizes, own_block * BLK, BLK)
    keep_mask = keep_rows[:, None] & keep_cols[None, :]
    masked = jnp.where(keep_mask[None], amplitudes, jnp.zeros_like(amplitudes))
    panels = lax.all_gather(masked, "ab", axis=1, tiled=True)
    first_irrep = row_first // per_irrep
    pieces = []
    for second in range(IRREPS):
        source = jnp.bitwise_xor(jnp.bitwise_xor(first_irrep, second), own_block)
        amp_block = lax.dynamic_slice_in_dim(panels, source * BLK, BLK, 1)
        row_block = integrals[:, second * per_irrep : (second + 1) * per_irrep]
        pieces.append(
            jnp.einsum("abcd,pcd->pab", row_block, amp_block, preferred_element_type=jnp.float32)
        )
    partial_sum = jnp.concatenate(pieces, axis=2)
    ladder = lax.psum(partial_sum, "cd")
    mirrored = lax.all_to_all(ladder, "ab", split_axis=2, concat_axis=1, tiled=True)
    return ladder + jnp.transpose(mirrored, (0, 2, 1))


def solution(mesh):
    placed = (P("ab", None, None, "cd"), P(None, "ab", "cd"), P())
    return jax.shard_map(
        on_device, mesh=mesh, in_specs=placed, out_specs=P(None, "ab", None), check_vma=False
    )
```

profile of v0, /device:TPU:0, one launch (start us, length us, event | category | flops | bytes accessed | tf_op | source)
XLA Modules:
  0.0 215.9 jit_solution(4799325225221977902)
XLA Ops:
  6.5 0.0 all-gather.2.cloned.1.call-start
  6.5 0.7 select_reduce_fusion
  7.3 0.7 select_reduce_fusion.1
  8.1 0.1 broadcast_and_fusion
  8.2 1.5 copy_select_fusion
  9.6 0.0 all-gather.2.cloned.1.call-update
  9.7 7.4 %fusion.34 = (bf16[3,24,128,128]{3,2,1,0:T(8,128)(2,1)}, bf16[3,24,128,128]{3,2,1,0:T(8,128)(2,1)}, bf16[3,24,128,128]{3,2,1,0:T(8,128)(2,1)}, bf16[3,24,128,128]{3,2,1,0:T(8,128)(2,1)S(1)}) fusion(bf16[3,96,128,128]{3,2,1,0:T(8,128)(2,1)} %param.3), kind=kLoop, calls=%fused_computation.46 | loop fusion | bytes 18874368 | tf_op jit(solution)/shard_map/slice | solution.py:37
  17.1 148.4 %all-gather.2.cloned.1.call-done = bf16[16,512,128]{2,0,1:T(8,128)(2,1)} async-done(((bf16[16,16,128]{2,0,1:T(8,128)(2,1)}), bf16[16,512,128]{2,0,1:T(8,128)(2,1)}) %all-gather.2.cloned.1.call-update) | async-done | bytes 2097168 | tf_op jit(solution)/shard_map/all_gather | solution.py:31
  165.5 0.0 copy-start.1
  165.5 3.7 %fusion.11 = f32[16,3,24]{2,0,1:T(8,128)S(1)} fusion(bf16[3,24,128,128]{3,2,1,0:T(8,128)(2,1)} %get-tuple-element.7, bf16[16,512,128]{2,0,1:T(8,128)(2,1)} %all-gather.2.cloned.1.call-done, s32[]{:T(128)S(6)} %select_n.76), kind=kOutput, calls=%fused_computation.9 | convolution fusion | flops 37748736 | bytes 2888196 | tf_op jit(solution)/shard_map/abcd,pcd->pab/dot_general | solution.py:39
  169.2 0.0 copy-start
  169.2 0.0 copy-done.1
  169.2 3.0 %fusion.8 = f32[16,3,24]{2,0,1:T(8,128)S(1)} fusion(bf16[3,24,128,128]{3,2,1,0:T(8,128)(2,1)S(1)} %copy-done.1, bf16[16,512,128]{2,0,1:T(8,128)(2,1)} %all-gather.2.cloned.1.call-done, s32[]{:T(128)S(6)} %select_n.75), kind=kOutput, calls=%fused_computation.8 | convolution fusion | flops 37748736 | bytes 2888196 | tf_op jit(solution)/shard_map/abcd,pcd->pab/dot_general | solution.py:39
  172.2 0.0 copy-done
  172.2 2.8 %fusion.14 = f32[16,3,24]{2,0,1:T(8,128)S(1)} fusion(bf16[3,24,128,128]{3,2,1,0:T(8,128)(2,1)S(1)} %copy-done, bf16[16,512,128]{2,0,1:T(8,128)(2,1)} %all-gather.2.cloned.1.call-done, s32[]{:T(128)S(6)} %select_n.77), kind=kOutput, calls=%fused_computation.10 | convolution fusion | flops 37748736 | bytes 2888196 | tf_op jit(solution)/shard_map/abcd,pcd->pab/dot_general | solution.py:39
  175.0 2.8 %fusion.17 = f32[16,3,24]{2,0,1:T(8,128)S(1)} fusion(bf16[3,24,128,128]{3,2,1,0:T(8,128)(2,1)S(1)} %get-tuple-element.8, bf16[16,512,128]{2,0,1:T(8,128)(2,1)} %all-gather.2.cloned.1.call-done, s32[]{:T(128)S(6)} %select_n.78), kind=kOutput, calls=%fused_computation.11 | convolution fusion | flops 37748736 | bytes 2888196 | tf_op jit(solution)/shard_map/abcd,pcd->pab/dot_general | solution.py:39
  177.8 0.1 pad_maximum_fusion
  177.9 13.3 %psum.7 = f32[16,3,96]{2,0,1:T(8,128)S(1)} all-reduce(f32[16,3,96]{2,0,1:T(8,128)S(1)} %pad_maximum_fusion), channel_id=1, replica_groups=mesh['ab'=32,'cd'=4] {'cd'}, use_global_device_ids=true, to_apply=%region_2.3 | all-reduce | flops 4608 | bytes 36864 | tf_op jit(solution)/shard_map/psum | solution.py:42
  191.2 0.1 copy.32
  191.3 0.2 reshape.108
  191.5 15.4 %all_to_all.18 = f32[32,1,144]{2,1,0:T(1,128)S(1)} all-to-all(f32[32,1,144]{2,1,0:T(1,128)S(1)} %reshape.108), channel_id=1, replica_groups=mesh['ab'=32,'cd'=4] {'ab'}, dimensions={0} | all-to-all | bytes 36864 | tf_op jit(solution)/shard_map/all_to_all | solution.py:43
  206.8 0.5 broadcast.182
  207.3 0.7 reduce
  208.1 0.1 reshape.109
  208.3 0.1 all_to_all.16
  208.3 0.1 copy.35
  208.4 0.6 bitcast_add_fusion
  (5 shorter events, 0.1 us)
Async XLA Ops:
  6.5 158.9 %all-gather.2.cloned.1.call-start = ((), (), s32[]{:S(2)}) async-start(), calls=%async_computation.1 | async-start | bytes 2162688 | tf_op jit(solution)/shard_map/all_gather | solution.py:31
  165.5 3.7 %copy-start.1 = (bf16[3,24,128,128]{3,2,1,0:T(8,128)(2,1)S(1)}, bf16[3,24,128,128]{3,2,1,0:T(8,128)(2,1)}, u32[]{:S(2)}) copy-start(bf16[3,24,128,128]{3,2,1,0:T(8,128)(2,1)} %get-tuple-element.5) | copy-start | bytes 7077892
  169.2 3.0 %copy-start = (bf16[3,24,128,128]{3,2,1,0:T(8,128)(2,1)S(1)}, bf16[3,24,128,128]{3,2,1,0:T(8,128)(2,1)}, u32[]{:S(2)}) copy-start(bf16[3,24,128,128]{3,2,1,0:T(8,128)(2,1)} %get-tuple-element.6) | copy-start | bytes 7077892
Sparse Core Ops, SparseCore 0:
  9.8 155.6 all-gather.1
where the time goes:
time: 216 us
  waiting for transfers between devices  148 us (69%)
  blocking collectives  28.6 us (13%)
  between operations  13.5 us (6%)
  matrix products  12.3 us (6%)
  local copies, waits for them, and re-layouts  8.51 us (4%)
  other arithmetic  4.54 us (2%)
    all_gather x1, waiting for transfers between devices, on_device(): panels = lax.all_gather(masked, 'ab', axis=1, tiled=True)  148 us
    all_to_all x1, blocking collectives, on_device(): lax.all_to_all(ladder, 'ab', split_axis=2, concat_axis=1, tiled=True)  15.4 us
    psum x1, blocking collectives, on_device(): ladder = lax.psum(partial_sum, 'cd')  13.3 us
    dot_general x4, matrix products, on_device(): jnp.einsum('abcd,pcd->pab', row_block, amp_block, preferred_element_type=...  12.3 us
    slice x1, local copies, waits for them, and re-layouts, on_device(): row_block = integrals[:, second * per_irrep:(second + 1) * per_irrep]  7.4 us
  transfers between devices with their start and end apart: 1, of which 1 were waited for; matrix products, arithmetic and copies ran while one was open for 3% of the time, Pallas kernels for 0%

commit v1 on v0

--- a/solution.py
+++ b/solution.py
@@ -28,7 +28,16 @@
     keep_cols = occupied_slots(block_sizes, own_block * BLK, BLK)
     keep_mask = keep_rows[:, None] & keep_cols[None, :]
     masked = jnp.where(keep_mask[None], amplitudes, jnp.zeros_like(amplitudes))
-    panels = lax.all_gather(masked, "ab", axis=1, tiled=True)
+    turn_case = lambda array_here, ax_name: jnp.concatenate(
+        lax.all_to_all(
+            jnp.stack([array_here for _ in range(lax.psum(1, axis_name=ax_name))]),
+            concat_axis=0,
+            split_axis=0,
+            axis_name=ax_name,
+        ),
+        axis=1,
+    )
+    panels = turn_case(masked, "ab")
     first_irrep = row_first // per_irrep
     pieces = []
     for second in range(IRREPS):

time: 216 us -> 87.2 us (0.40)
  waiting for transfers between devices: 148 us -> 20.9 us
  between operations: 13.5 us -> 0.13 us
  starting transfers between devices: 0.01 us -> 9.39 us
    all_gather x1 -> x0, waiting for transfers between devices: 148 us -> none  [on_device(): panels = lax.all_gather(masked, 'ab', axis=1, tiled=True)]
    all_to_all x0 -> x1, waiting for transfers between devices: none -> 20.9 us  [on_device(): lax.all_to_all(jnp.stack([array_here for _ in range(lax.psum(1, axis_name...]
    all_to_all x0 -> x1, starting transfers between devices: none -> 9.39 us  [on_device(): lax.all_to_all(jnp.stack([array_here for _ in range(lax.psum(1, axis_name...]
  transfers between devices with their start and end apart: 1 -> 1, of which waited for: 1 -> 1; matrix products, arithmetic and copies ran while one was open for 3% -> 9% of each run, Pallas kernels for 0% -> 0%
where the time goes in v1:
time: 87.2 us; the launch traced here: 86.7 us
  blocking collectives  29.8 us (34%)
  waiting for transfers between devices  20.9 us (24%)
  matrix products  12.3 us (14%)
  local copies, waits for them, and re-layouts  10.3 us (12%)
  starting transfers between devices  9.39 us (11%)
  other arithmetic  3.91 us (4%)
    all_to_all x1, waiting for transfers between devices, on_device(): lax.all_to_all(jnp.stack([array_here for _ in range(lax.psum(1, axis_name...  20.9 us
    all_to_all x1, blocking collectives, on_device(): lax.all_to_all(ladder, 'ab', split_axis=2, concat_axis=1, tiled=True)  15.3 us
    psum x1, blocking collectives, on_device(): ladder = lax.psum(partial_sum, 'cd')  14.5 us
    dot_general x4, matrix products, on_device(): jnp.einsum('abcd,pcd->pab', row_block, amp_block, preferred_element_type=...  12.3 us
    all_to_all x1, starting transfers between devices, on_device(): lax.all_to_all(jnp.stack([array_here for _ in range(lax.psum(1, axis_name...  9.39 us
    slice x1, local copies, waits for them, and re-layouts, on_device(): row_block = integrals[:, second * per_irrep:(second + 1) * per_irrep]  7.4 us
    another operation x1, local copies, waits for them, and re-layouts, on_device(): jnp.stack([array_here for _ in range(lax.psum(1, axis_name=ax_name))])  1.79 us
  transfers between devices with their start and end apart: 1, of which 1 were waited for; matrix products, arithmetic and copies ran while one was open for 9% of the time, Pallas kernels for 0%

profile of v1, /device:TPU:0, one launch (start us, length us, event | category | flops | bytes accessed | tf_op | source)
XLA Modules:
  0.0 86.7 jit_solution(7791773805467734397)
XLA Ops:
  0.0 0.7 select_reduce_fusion
  0.8 0.7 select_reduce_fusion.1
  1.5 0.1 broadcast_and_fusion
  1.6 0.8 broadcast_select_fusion
  2.5 1.8 %stack.2 = bf16[32,16,16,128]{3,1,2,0:T(8,128)(2,1)} broadcast(bf16[16,16,128]{2,0,1:T(8,128)(2,1)S(1)} %copy.27), dimensions={1,2,3} | broadcast | bytes 2162688 | tf_op jit(solution)/shard_map/stack | solution.py:33
  4.3 9.4 %all-to-all-start = ((bf16[32,16,16,128]{3,1,2,0:T(8,128)(2,1)}), bf16[32,16,16,128]{3,1,2,0:T(8,128)(2,1)}, u32[]{:S(2)}, u32[]{:S(2)}) async-start(bf16[32,16,16,128]{3,1,2,0:T(8,128)(2,1)} %stack.2), calls=%async_computation | async-start | bytes 4194304 | tf_op jit(solution)/shard_map/all_to_all | solution.py:32
  13.7 7.4 %fusion.34 = (bf16[3,24,128,128]{3,2,1,0:T(8,128)(2,1)}, bf16[3,24,128,128]{3,2,1,0:T(8,128)(2,1)}, bf16[3,24,128,128]{3,2,1,0:T(8,128)(2,1)}, bf16[3,24,128,128]{3,2,1,0:T(8,128)(2,1)S(1)}) fusion(bf16[3,96,128,128]{3,2,1,0:T(8,128)(2,1)} %param.3), kind=kLoop, calls=%fused_computation.46 | loop fusion | bytes 18874368 | tf_op jit(solution)/shard_map/slice | solution.py:46
  21.1 20.9 %all-to-all-done = bf16[32,16,16,128]{3,1,2,0:T(8,128)(2,1)} async-done(((bf16[32,16,16,128]{3,1,2,0:T(8,128)(2,1)}), bf16[32,16,16,128]{3,1,2,0:T(8,128)(2,1)}, u32[]{:S(2)}, u32[]{:S(2)}) %all-to-all-start) | async-done | bytes 2097184 | tf_op jit(solution)/shard_map/all_to_all | solution.py:32
  42.0 0.0 copy-start.1
  42.0 3.7 %fusion.11 = f32[16,3,24]{2,0,1:T(8,128)S(1)} fusion(bf16[3,24,128,128]{3,2,1,0:T(8,128)(2,1)} %get-tuple-element.7, bf16[16,512,128]{2,0,1:T(8,128)(2,1)} %bitcast.1, s32[]{:T(128)S(6)} %select_n.76), kind=kOutput, calls=%fused_computation.9 | convolution fusion | flops 37748736 | bytes 2888196 | tf_op jit(solution)/shard_map/abcd,pcd->pab/dot_general | solution.py:48
  45.7 0.0 copy-start
  45.7 0.0 copy-done.1
  45.7 3.0 %fusion.8 = f32[16,3,24]{2,0,1:T(8,128)S(1)} fusion(bf16[3,24,128,128]{3,2,1,0:T(8,128)(2,1)S(1)} %copy-done.1, bf16[16,512,128]{2,0,1:T(8,128)(2,1)} %bitcast.1, s32[]{:T(128)S(6)} %select_n.75), kind=kOutput, calls=%fused_computation.8 | convolution fusion | flops 37748736 | bytes 2888196 | tf_op jit(solution)/shard_map/abcd,pcd->pab/dot_general | solution.py:48
  48.7 0.0 copy-done
  48.7 2.8 %fusion.14 = f32[16,3,24]{2,0,1:T(8,128)S(1)} fusion(bf16[3,24,128,128]{3,2,1,0:T(8,128)(2,1)S(1)} %copy-done, bf16[16,512,128]{2,0,1:T(8,128)(2,1)} %bitcast.1, s32[]{:T(128)S(6)} %select_n.77), kind=kOutput, calls=%fused_computation.10 | convolution fusion | flops 37748736 | bytes 2888196 | tf_op jit(solution)/shard_map/abcd,pcd->pab/dot_general | solution.py:48
  51.6 2.8 %fusion.17 = f32[16,3,24]{2,0,1:T(8,128)S(1)} fusion(bf16[3,24,128,128]{3,2,1,0:T(8,128)(2,1)S(1)} %get-tuple-element.8, bf16[16,512,128]{2,0,1:T(8,128)(2,1)} %bitcast.1, s32[]{:T(128)S(6)} %select_n.78), kind=kOutput, calls=%fused_computation.11 | convolution fusion | flops 37748736 | bytes 2888196 | tf_op jit(solution)/shard_map/abcd,pcd->pab/dot_general | solution.py:48
  54.3 0.1 pad_maximum_fusion
  54.4 14.5 %psum.7 = f32[16,3,96]{2,0,1:T(8,128)S(1)} all-reduce(f32[16,3,96]{2,0,1:T(8,128)S(1)} %pad_maximum_fusion), channel_id=1, replica_groups=mesh['ab'=32,'cd'=4] {'cd'}, use_global_device_ids=true, to_apply=%region_2.3 | all-reduce | flops 4608 | bytes 36864 | tf_op jit(solution)/shard_map/psum | solution.py:51
  68.9 0.1 copy.32
  69.1 0.2 reshape.118
  69.2 15.3 %all_to_all.23 = f32[32,1,144]{2,1,0:T(1,128)S(1)} all-to-all(f32[32,1,144]{2,1,0:T(1,128)S(1)} %reshape.118), channel_id=1, replica_groups=mesh['ab'=32,'cd'=4] {'ab'}, dimensions={0} | all-to-all | bytes 36864 | tf_op jit(solution)/shard_map/all_to_all | solution.py:52
  84.5 0.5 broadcast.184
  85.0 0.7 reduce
  85.8 0.1 reshape.119
  86.0 0.1 all_to_all.20
  86.0 0.1 copy.35
  86.1 0.6 bitcast_add_fusion
  (6 shorter events, 0.1 us)
Async XLA Ops:
  4.3 37.7 %all-to-all-start = ((bf16[32,16,16,128]{3,1,2,0:T(8,128)(2,1)}), bf16[32,16,16,128]{3,1,2,0:T(8,128)(2,1)}, u32[]{:S(2)}, u32[]{:S(2)}) async-start(bf16[32,16,16,128]{3,1,2,0:T(8,128)(2,1)} %stack.2), calls=%async_computation | async-start | bytes 4194304 | tf_op jit(solution)/shard_map/all_to_all | solution.py:32
  42.0 3.7 %copy-start.1 = (bf16[3,24,128,128]{3,2,1,0:T(8,128)(2,1)S(1)}, bf16[3,24,128,128]{3,2,1,0:T(8,128)(2,1)}, u32[]{:S(2)}) copy-start(bf16[3,24,128,128]{3,2,1,0:T(8,128)(2,1)} %get-tuple-element.5) | copy-start | bytes 7077892
  45.7 3.0 %copy-start = (bf16[3,24,128,128]{3,2,1,0:T(8,128)(2,1)S(1)}, bf16[3,24,128,128]{3,2,1,0:T(8,128)(2,1)}, u32[]{:S(2)}) copy-start(bf16[3,24,128,128]{3,2,1,0:T(8,128)(2,1)} %get-tuple-element.6) | copy-start | bytes 7077892

commit v2 on v0

--- a/solution.py
+++ b/solution.py
@@ -39,7 +39,8 @@
             jnp.einsum("abcd,pcd->pab", row_block, amp_block, preferred_element_type=jnp.float32)
         )
     partial_sum = jnp.concatenate(pieces, axis=2)
-    ladder = lax.psum(partial_sum, "cd")
+    parts = lax.all_gather(partial_sum, "cd", axis=0, tiled=False)
+    ladder = parts.sum(axis=0)
     mirrored = lax.all_to_all(ladder, "ab", split_axis=2, concat_axis=1, tiled=True)
     return ladder + jnp.transpose(mirrored, (0, 2, 1))
 

time: 216 us -> 210 us (0.972)
  blocking collectives: 28.6 us -> 22.2 us
    psum x1 -> x0, blocking collectives: 13.3 us -> none  [on_device(): ladder = lax.psum(partial_sum, 'cd')]
    all_gather x0 -> x1, blocking collectives: none -> 6.84 us  [on_device(): parts = lax.all_gather(partial_sum, 'cd', axis=0, tiled=False)]
  transfers between devices with their start and end apart: 1 -> 1, of which waited for: 1 -> 1; matrix products, arithmetic and copies ran while one was open for 3% -> 4% of each run, Pallas kernels for 0% -> 0%
where the time goes in v2:
time: 210 us; the launch traced here: 209 us
  waiting for transfers between devices  148 us (70%)
  blocking collectives  22.2 us (11%)
  between operations  13.5 us (6%)
  matrix products  12.3 us (6%)
  local copies, waits for them, and re-layouts  8.51 us (4%)
  other arithmetic  4.56 us (2%)
    all_gather x1, waiting for transfers between devices, on_device(): panels = lax.all_gather(masked, 'ab', axis=1, tiled=True)  148 us
    all_to_all x1, blocking collectives, on_device(): lax.all_to_all(ladder, 'ab', split_axis=2, concat_axis=1, tiled=True)  15.4 us
    dot_general x4, matrix products, on_device(): jnp.einsum('abcd,pcd->pab', row_block, amp_block, preferred_element_type=...  12.3 us
    slice x1, local copies, waits for them, and re-layouts, on_device(): row_block = integrals[:, second * per_irrep:(second + 1) * per_irrep]  7.4 us
    all_gather x1, blocking collectives, on_device(): parts = lax.all_gather(partial_sum, 'cd', axis=0, tiled=False)  6.84 us
  transfers between devices with their start and end apart: 1, of which 1 were waited for; matrix products, arithmetic and copies ran while one was open for 4% of the time, Pallas kernels for 0%

profile of v2, /device:TPU:0, one launch (start us, length us, event | category | flops | bytes accessed | tf_op | source)
XLA Modules:
  0.0 209.5 jit_solution(13628820816592851074)
XLA Ops:
  6.5 0.0 all-gather.3.cloned.1.call-start
  6.5 0.7 select_reduce_fusion
  7.3 0.7 select_reduce_fusion.1
  8.1 0.1 broadcast_and_fusion
  8.2 1.5 copy_select_fusion
  9.6 0.0 all-gather.3.cloned.1.call-update
  9.7 7.4 %fusion.34 = (bf16[3,24,128,128]{3,2,1,0:T(8,128)(2,1)}, bf16[3,24,128,128]{3,2,1,0:T(8,128)(2,1)}, bf16[3,24,128,128]{3,2,1,0:T(8,128)(2,1)}, bf16[3,24,128,128]{3,2,1,0:T(8,128)(2,1)S(1)}) fusion(bf16[3,96,128,128]{3,2,1,0:T(8,128)(2,1)} %param.3), kind=kLoop, calls=%fused_computation.46 | loop fusion | bytes 18874368 | tf_op jit(solution)/shard_map/slice | solution.py:37
  17.1 148.4 %all-gather.3.cloned.1.call-done = bf16[16,512,128]{2,0,1:T(8,128)(2,1)} async-done(((bf16[16,16,128]{2,0,1:T(8,128)(2,1)}), bf16[16,512,128]{2,0,1:T(8,128)(2,1)}) %all-gather.3.cloned.1.call-update) | async-done | bytes 2097168 | tf_op jit(solution)/shard_map/all_gather | solution.py:31
  165.5 0.0 copy-start.1
  165.5 3.7 %fusion.11 = f32[16,3,24]{2,0,1:T(8,128)S(1)} fusion(bf16[3,24,128,128]{3,2,1,0:T(8,128)(2,1)} %get-tuple-element.7, bf16[16,512,128]{2,0,1:T(8,128)(2,1)} %all-gather.3.cloned.1.call-done, s32[]{:T(128)S(6)} %select_n.76), kind=kOutput, calls=%fused_computation.9 | convolution fusion | flops 37748736 | bytes 2888196 | tf_op jit(solution)/shard_map/abcd,pcd->pab/dot_general | solution.py:39
  169.2 0.0 copy-start
  169.2 0.0 copy-done.1
  169.2 3.0 %fusion.8 = f32[16,3,24]{2,0,1:T(8,128)S(1)} fusion(bf16[3,24,128,128]{3,2,1,0:T(8,128)(2,1)S(1)} %copy-done.1, bf16[16,512,128]{2,0,1:T(8,128)(2,1)} %all-gather.3.cloned.1.call-done, s32[]{:T(128)S(6)} %select_n.75), kind=kOutput, calls=%fused_computation.8 | convolution fusion | flops 37748736 | bytes 2888196 | tf_op jit(solution)/shard_map/abcd,pcd->pab/dot_general | solution.py:39
  172.2 0.0 copy-done
  172.2 2.8 %fusion.14 = f32[16,3,24]{2,0,1:T(8,128)S(1)} fusion(bf16[3,24,128,128]{3,2,1,0:T(8,128)(2,1)S(1)} %copy-done, bf16[16,512,128]{2,0,1:T(8,128)(2,1)} %all-gather.3.cloned.1.call-done, s32[]{:T(128)S(6)} %select_n.77), kind=kOutput, calls=%fused_computation.10 | convolution fusion | flops 37748736 | bytes 2888196 | tf_op jit(solution)/shard_map/abcd,pcd->pab/dot_general | solution.py:39
  175.0 2.8 %fusion.17 = f32[16,3,24]{2,0,1:T(8,128)S(1)} fusion(bf16[3,24,128,128]{3,2,1,0:T(8,128)(2,1)S(1)} %get-tuple-element.8, bf16[16,512,128]{2,0,1:T(8,128)(2,1)} %all-gather.3.cloned.1.call-done, s32[]{:T(128)S(6)} %select_n.78), kind=kOutput, calls=%fused_computation.11 | convolution fusion | flops 37748736 | bytes 2888196 | tf_op jit(solution)/shard_map/abcd,pcd->pab/dot_general | solution.py:39
  177.8 0.1 pad_maximum_fusion
  177.9 6.8 %all-gather = f32[64,3,96]{2,0,1:T(8,128)S(1)} all-gather(f32[16,3,96]{2,0,1:T(8,128)S(1)} %pad_maximum_fusion), channel_id=2, replica_groups=mesh['ab'=32,'cd'=4] {'cd'}, dimensions={0}, use_global_device_ids=true | all-gather | bytes 92160 | tf_op jit(solution)/shard_map/all_gather | solution.py:42
  184.8 0.1 copy.31
  184.9 0.2 reshape.109
  185.0 15.4 %all_to_all.18 = f32[32,1,144]{2,1,0:T(1,128)S(1)} all-to-all(f32[32,1,144]{2,1,0:T(1,128)S(1)} %reshape.109), channel_id=1, replica_groups=mesh['ab'=32,'cd'=4] {'ab'}, dimensions={0} | all-to-all | bytes 36864 | tf_op jit(solution)/shard_map/all_to_all | solution.py:44
  200.4 0.5 broadcast.182
  200.9 0.7 reduce
  201.7 0.1 reshape.110
  201.8 0.1 all_to_all.16
  201.9 0.1 copy.34
  202.0 0.6 bitcast_add_fusion
  (6 shorter events, 0.1 us)
Async XLA Ops:
  6.5 158.9 %all-gather.3.cloned.1.call-start = ((), (), s32[]{:S(2)}) async-start(), calls=%async_computation.1 | async-start | bytes 2162688 | tf_op jit(solution)/shard_map/all_gather | solution.py:31
  165.5 3.7 %copy-start.1 = (bf16[3,24,128,128]{3,2,1,0:T(8,128)(2,1)S(1)}, bf16[3,24,128,128]{3,2,1,0:T(8,128)(2,1)}, u32[]{:S(2)}) copy-start(bf16[3,24,128,128]{3,2,1,0:T(8,128)(2,1)} %get-tuple-element.5) | copy-start | bytes 7077892
  169.2 3.0 %copy-start = (bf16[3,24,128,128]{3,2,1,0:T(8,128)(2,1)S(1)}, bf16[3,24,128,128]{3,2,1,0:T(8,128)(2,1)}, u32[]{:S(2)}) copy-start(bf16[3,24,128,128]{3,2,1,0:T(8,128)(2,1)} %get-tuple-element.6) | copy-start | bytes 7077892
Sparse Core Ops, SparseCore 0:
  9.8 155.6 all-gather.2
